TPU v7x, 32 devices: a whole 2x2x4 slice. The times are simulated.
32 devices in a mesh: colony: 8 (over z, y), fsdp: 4 (over x, core).
Axes of the slice: x: 2, y: 2, z: 4, core: 2. Of those that a mesh axis runs over, the one named last changes fastest.
Arguments:
- hidden_states: bfloat16 [8, 512, 4096], P('colony', 'fsdp'), may hold values from -40 to 40
- norm_gain: float32 [4096], replicated, may hold values from 0.25 to 1.75
- gate_weight: bfloat16 [4096, 7168], P(None, 'fsdp'), may hold values from -0.09375 to 0.09375
- up_weight: bfloat16 [4096, 7168], P(None, 'fsdp'), may hold values from -0.09375 to 0.09375
- hidden_grad: bfloat16 [8, 512, 7168], P('colony', 'fsdp'), may hold values from -2 to 2
- byz_order: int32 [8], replicated, may hold values from 0 to 7, each once
- byz_scale: float32 [3], replicated, may hold values from 2 to 6
Outputs:
- median_gate: float32 [4096, 7168], P('colony', 'fsdp')
- median_up: float32 [4096, 7168], P('colony', 'fsdp')
All inputs are finite; a program needn't handle non-finite values.
Results may differ from a plain program's by a relative error of at most 0.002.
The roundings to bfloat16 on the way count: a program that leaves them out, or rounds other values in their place, can miss the bound.
Values may be sent and summed in bfloat16 or wider, within the bound.
No kernel may reach another device: no remote copies, remote signals or barrier semaphores. Data moves between devices by JAX's collectives and lax.ppermute only.
A program may use at most 192 MiB of HBM per device.

v0:
```python
import jax
import jax.numpy as jnp
from jax import lax
from jax.sharding import PartitionSpec as P

NBYZ = 3
ITERS = 3


def backward_grads(normed_all, cotangent, gate_weight, up_weight):
    gate = jnp.dot(normed_all, gate_weight, preferred_element_type=jnp.float32)
    up = jnp.dot(normed_all, up_weight, preferred_element_type=jnp.float32)
    sig = jax.nn.sigmoid(gate)
    back = cotangent.astype(jnp.float32)
    d_up = (back * gate * sig).astype(jnp.bfloat16)
    d_gate = (back * up * sig * (1.0 + gate * (1.0 - sig))).astype(jnp.bfloat16)
    return (d_gate, d_up)


def token_contract(normed_all, delta):
    dims = (((0,), (0,)), ((), ()))
    return lax.dot_general(normed_all, delta, dims, preferred_element_type=jnp.float32).astype(
        jnp.bfloat16
    )


def on_device(hidden_states, norm_gain, gate_weight, up_weight, hidden_grad, byz_order, byz_scale):
    values = hidden_states[0].astype(jnp.float32)
    meansq = jnp.mean(values * values, axis=-1, keepdims=True)
    normed = (values * lax.rsqrt(meansq + 1e-05) * norm_gain).astype(jnp.bfloat16)
    normed_all = lax.all_gather(normed, "fsdp", axis=0, tiled=True)
    cotangent = lax.all_to_all(hidden_grad[0], "fsdp", split_axis=1, concat_axis=0, tiled=True)
    d_gate, d_up = backward_grads(normed_all, cotangent, gate_weight, up_weight)
    grad_gate = token_contract(normed_all, d_gate)
    grad_up = token_contract(normed_all, d_up)
    stacked = jnp.stack([grad_gate, grad_up])[None]
    pieces = lax.all_to_all(stacked, "colony", split_axis=2, concat_axis=0, tiled=True)
    count = lax.axis_size("colony")
    colonies = jnp.arange(count, dtype=jnp.int32)
    hits = byz_order[:NBYZ][:, None] == colonies[None, :]
    factor = 1.0 + jnp.sum(jnp.where(hits, -byz_scale[:, None] - 1.0, jnp.float32(0.0)), axis=0)

    def combine(coef):
        return jnp.sum(coef[:, None, None, None] * pieces.astype(jnp.float32), axis=0)

    median = combine(factor / count)
    for step in range(ITERS):
        diff = factor[:, None, None, None] * pieces.astype(jnp.float32) - median[None]
        partial_value = jnp.sum(diff * diff, axis=(1, 2, 3))
        dist = jnp.sqrt(lax.psum(partial_value, ("colony", "fsdp")) + 1e-06)
        weights = 1.0 / dist
        median = combine(weights * factor / jnp.sum(weights))
    return (median[0], median[1])


def solution(mesh):
    placed = (
        P("colony", "fsdp", None),
        P(),
        P(None, "fsdp"),
        P(None, "fsdp"),
        P("colony", "fsdp", None),
        P(),
        P(),
    )
    return jax.shard_map(
        on_device,
        mesh=mesh,
        in_specs=placed,
        out_specs=(P("colony", "fsdp"), P("colony", "fsdp")),
        check_vma=False,
    )
```

profile of v0, /device:TPU:0, one launch (start us, length us, event | category | flops | bytes accessed | tf_op | source)
XLA Modules:
  0.0 1383.5 jit_solution(15164193950256069921)
XLA Ops:
  8.7 2.5 fusion.22
  11.3 3.6 all_to_all.7
  15.1 44.7 %all_to_all.22 = bf16[128,4,1792]{2,0,1:T(8,128)(2,1)S(1)} all-to-all(bf16[128,4,1792]{2,0,1:T(8,128)(2,1)S(1)} %copy.14), channel_id=1, replica_groups=mesh['colony'=8,'fsdp'=4] {'fsdp'}, dimensions={1} | all-to-all | bytes 3670016 | tf_op jit(solution)/shard_map/all_to_all | solution.py:32
  59.8 6.3 all-gather.2.cloned.1.call-done
  66.1 15.8 %fusion.19 = (bf16[512,1792]{1,0:T(8,128)(2,1)S(1)}, f32[512,1792]{1,0:T(8,128)S(1)}) fusion(bf16[128,4,1792]{2,0,1:T(8,128)(2,1)S(1)} %all_to_all.22, bf16[512,4096]{1,0:T(8,128)(2,1)} %all-gather.2.cloned.1.call-done, bf16[4096,1792]{1,0:T(8,128)(2,1)} %param.9), kind=kOutput, calls=%fused_computation.31 | convolution fusion | flops 7522615296 | bytes 26214400 | tf_op jit(solution)/shard_map/dot_general | solution.py:11
  81.9 12.9 fusion.17
  94.9 11.1 fusion.13
  105.9 11.3 fusion.14
  117.3 20.6 %maximum_bitcast_fusion = bf16[1,2,4096,1792]{3,2,1,0:T(8,128)(2,1)} fusion(bf16[1,4096,1792]{2,1,0:T(8,128)(2,1)} %fusion.14, bf16[1,4096,1792]{2,1,0:T(8,128)(2,1)} %fusion.13), kind=kLoop, calls=%fused_computation.18 | loop fusion | flops 14680064 | bytes 58720256 | tf_op jit(solution)/shard_map/broadcast_in_dim | solution.py:36
  137.9 53.1 %copy.15 = bf16[1,2,4096,1792]{3,1,0,2:T(2,128)(2,1)} copy(bf16[1,2,4096,1792]{3,2,1,0:T(8,128)(2,1)} %maximum_bitcast_fusion) | data formatting | bytes 58720256 | tf_op jit(solution)/shard_map/broadcast_in_dim | solution.py:36
  191.0 6.9 all-to-all-start.1
  198.1 633.0 %all-to-all-done.1 = bf16[1,2,4096,1792]{3,1,0,2:T(2,128)(2,1)} async-done(((bf16[1,2,4096,1792]{3,1,0,2:T(2,128)(2,1)}), bf16[1,2,4096,1792]{3,1,0,2:T(2,128)(2,1)}, u32[]{:S(2)}, u32[]{:S(2)}) %all-to-all-start.1) | async-done | bytes 29360160 | tf_op jit(solution)/shard_map/all_to_all | solution.py:37
  831.1 60.1 %fusion.6 = f32[2,512,1792]{2,0,1:T(2,128)S(1)} fusion(bf16[1,2,8,512,1792]{4,1,3,2,0:T(2,128)(2,1)} %bitcast.11, f32[8]{0:T(128)S(1)} %get-tuple-element.4), kind=kLoop, calls=%fused_computation.11 | loop fusion | flops 42205184 | bytes 36700192 | tf_op jit(solution)/shard_map/reduce_sum | solution.py:44
  891.2 57.7 %fusion.12 = f32[8]{0:T(128)S(1)} fusion(bf16[1,2,8,512,1792]{4,1,3,2,0:T(2,128)(2,1)} %bitcast.11, f32[8]{0:T(128)S(1)} %get-tuple-element.5, f32[2,512,1792]{2,0,1:T(2,128)S(1)} %fusion.6), kind=kLoop, calls=%fused_computation.17 | loop fusion | flops 73400312 | bytes 36700224 | tf_op jit(solution)/shard_map/reduce_sum | solution.py:49
  948.9 37.9 %psum.21 = f32[8]{0:T(128)S(1)} all-reduce(f32[8]{0:T(128)S(1)} %fusion.12), channel_id=1, replica_groups=mesh['colony'=8,'fsdp'=4] {'colony','fsdp'}, use_global_device_ids=true, to_apply=%region_4.5 | all-reduce | flops 8 | bytes 64 | tf_op jit(solution)/shard_map/psum | solution.py:50
  988.1 60.1 %fusion.7 = f32[2,512,1792]{2,0,1:T(2,128)S(1)} fusion(bf16[1,2,8,512,1792]{4,1,3,2,0:T(2,128)(2,1)} %bitcast.11, f32[8]{0:T(128)S(1)} %multiply_divide_fusion.2), kind=kLoop, calls=%fused_computation.12 | loop fusion | flops 42205184 | bytes 36700192 | tf_op jit(solution)/shard_map/reduce_sum | solution.py:44
  1048.1 57.7 %fusion.11 = f32[8]{0:T(128)S(1)} fusion(bf16[1,2,8,512,1792]{4,1,3,2,0:T(2,128)(2,1)} %bitcast.11, f32[8]{0:T(128)S(1)} %get-tuple-element.5, f32[2,512,1792]{2,0,1:T(2,128)S(1)} %fusion.7), kind=kLoop, calls=%fused_computation.16 | loop fusion | flops 73400312 | bytes 36700224 | tf_op jit(solution)/shard_map/reduce_sum | solution.py:49
  1105.9 41.7 %psum.22 = f32[8]{0:T(128)S(1)} all-reduce(f32[8]{0:T(128)S(1)} %fusion.11), channel_id=1, replica_groups=mesh['colony'=8,'fsdp'=4] {'colony','fsdp'}, use_global_device_ids=true, to_apply=%region_8.9 | all-reduce | flops 8 | bytes 64 | tf_op jit(solution)/shard_map/psum | solution.py:50
  1148.8 60.1 %fusion.8 = f32[2,512,1792]{2,0,1:T(2,128)S(1)} fusion(bf16[1,2,8,512,1792]{4,1,3,2,0:T(2,128)(2,1)} %bitcast.11, f32[8]{0:T(128)S(1)} %multiply_divide_fusion.1), kind=kLoop, calls=%fused_computation.13 | loop fusion | flops 42205184 | bytes 36700192 | tf_op jit(solution)/shard_map/reduce_sum | solution.py:44
  1208.9 57.7 %fusion.10 = f32[8]{0:T(128)S(1)} fusion(bf16[1,2,8,512,1792]{4,1,3,2,0:T(2,128)(2,1)} %bitcast.11, f32[8]{0:T(128)S(1)} %get-tuple-element.5, f32[2,512,1792]{2,0,1:T(2,128)S(1)} %fusion.8), kind=kLoop, calls=%fused_computation.15 | loop fusion | flops 73400312 | bytes 36700224 | tf_op jit(solution)/shard_map/reduce_sum | solution.py:49
  1266.6 38.8 %psum.23 = f32[8]{0:T(128)S(1)} all-reduce(f32[8]{0:T(128)S(1)} %fusion.10), channel_id=1, replica_groups=mesh['colony'=8,'fsdp'=4] {'colony','fsdp'}, use_global_device_ids=true, to_apply=%region_12.13 | all-reduce | flops 8 | bytes 64 | tf_op jit(solution)/shard_map/psum | solution.py:50
  1306.7 60.1 %fusion.9 = f32[2,512,1792]{2,0,1:T(2,128)S(1)} fusion(bf16[1,2,8,512,1792]{4,1,3,2,0:T(2,128)(2,1)} %bitcast.11, f32[8]{0:T(128)S(1)} %multiply_divide_fusion), kind=kLoop, calls=%fused_computation.14 | loop fusion | flops 42205184 | bytes 36700192 | tf_op jit(solution)/shard_map/reduce_sum | solution.py:44
  1366.8 5.8 fusion.26
  1372.6 3.5 copy_bitcast_fusion
  (20 shorter events, 5.6 us)
Async XLA Ops:
  7.2 58.9 %all-gather.2.cloned.1.call-start = ((), (), s32[]{:S(2)}) async-start(), calls=%async_computation.2 | async-start | bytes 5242880 | tf_op jit(solution)/shard_map/all_gather | solution.py:31
  66.1 15.8 %copy-start = (bf16[512,4096]{1,0:T(8,128)(2,1)S(1)}, bf16[512,4096]{1,0:T(8,128)(2,1)}, u32[]{:S(2)}) copy-start(bf16[512,4096]{1,0:T(8,128)(2,1)} %all-gather.2.cloned.1.call-done) | copy-start | bytes 12582916
  191.0 6.9 copy-start.1
  191.0 6.9 copy-start.2
  191.0 640.1 %all-to-all-start.1 = ((bf16[1,2,4096,1792]{3,1,0,2:T(2,128)(2,1)}), bf16[1,2,4096,1792]{3,1,0,2:T(2,128)(2,1)}, u32[]{:S(2)}, u32[]{:S(2)}) async-start(bf16[1,2,4096,1792]{3,1,0,2:T(2,128)(2,1)} %copy.15), calls=%async_computation.1 | async-start | bytes 58720256 | tf_op jit(solution)/shard_map/all_to_all | solution.py:37
Sparse Core Ops, SparseCore 0:
  11.4 54.6 all-gather.1
where the time goes:
time: 1400 us; the launch traced here: 1380 us
  waiting for transfers between devices  639 us (46%)
  other arithmetic  442 us (32%)
  blocking collectives  163 us (12%)
  local copies, waits for them, and re-layouts  66.3 us (5%)
  matrix products  51.2 us (4%)
  between operations  14.7 us (1%)
    all_to_all x1, waiting for transfers between devices, on_device(): lax.all_to_all(stacked, 'colony', split_axis=2, concat_axis=0, tiled=True)  633 us
    reduce_sum x4, other arithmetic, combine(): jnp.sum(coef[:, None, None, None] * pieces.astype(jnp.float32), axis=0)  240 us
    reduce_sum x3, other arithmetic, on_device(): partial_value = jnp.sum(diff * diff, axis=(1, 2, 3))  173 us
    psum x3, blocking collectives, on_device(): dist = jnp.sqrt(lax.psum(partial_value, ('colony', 'fsdp')) + 1e-06)  118 us
    broadcast_in_dim x1, local copies, waits for them, and re-layouts, on_device(): stacked = jnp.stack([grad_gate, grad_up])[None]  53.1 us
    all_to_all x1, blocking collectives, on_device(): lax.all_to_all(hidden_grad[0], 'fsdp', split_axis=1, concat_axis=0, tiled...  44.7 us
  transfers between devices with their start and end apart: 2, of which 2 were waited for; matrix products, arithmetic and copies ran while one was open for 0% of the time, Pallas kernels for 0%

commit v1 on v0

--- a/solution.py
+++ b/solution.py
@@ -47,7 +47,7 @@
     for step in range(ITERS):
         diff = factor[:, None, None, None] * pieces.astype(jnp.float32) - median[None]
         partial_value = jnp.sum(diff * diff, axis=(1, 2, 3))
-        dist = jnp.sqrt(lax.psum(partial_value, ("colony", "fsdp")) + 1e-06)
+        dist = jnp.sqrt(lax.psum(lax.psum(partial_value, "fsdp"), "colony") + 1e-06)
         weights = 1.0 / dist
         median = combine(weights * factor / jnp.sum(weights))
     return (median[0], median[1])

time: 1400 us -> 1350 us (0.964)
  blocking collectives: 163 us -> 118 us
    psum x3 -> x6, blocking collectives: 118 us -> 73.4 us  [on_device(): dist = jnp.sqrt(lax.psum(lax.psum(partial_value, 'fsdp'), 'colony') + 1e-06)]
where the time goes in v1:
time: 1350 us; the launch traced here: 1340 us
  waiting for transfers between devices  639 us (47%)
  other arithmetic  442 us (33%)
  blocking collectives  118 us (9%)
  local copies, waits for them, and re-layouts  66.3 us (5%)
  matrix products  51.2 us (4%)
  between operations  14.7 us (1%)
    all_to_all x1, waiting for transfers between devices, on_device(): lax.all_to_all(stacked, 'colony', split_axis=2, concat_axis=0, tiled=True)  633 us
    reduce_sum x4, other arithmetic, combine(): jnp.sum(coef[:, None, None, None] * pieces.astype(jnp.float32), axis=0)  240 us
    reduce_sum x3, other arithmetic, on_device(): partial_value = jnp.sum(diff * diff, axis=(1, 2, 3))  173 us
    psum x6, blocking collectives, on_device(): dist = jnp.sqrt(lax.psum(lax.psum(partial_value, 'fsdp'), 'colony') + 1e-06)  73.4 us
    broadcast_in_dim x1, local copies, waits for them, and re-layouts, on_device(): stacked = jnp.stack([grad_gate, grad_up])[None]  53.1 us
    all_to_all x1, blocking collectives, on_device(): lax.all_to_all(hidden_grad[0], 'fsdp', split_axis=1, concat_axis=0, tiled...  44.7 us
  transfers between devices with their start and end apart: 2, of which 2 were waited for; matrix products, arithmetic and copies ran while one was open for 0% of the time, Pallas kernels for 0%

profile of v1, /device:TPU:0, one launch (start us, length us, event | category | flops | bytes accessed | tf_op | source)
XLA Modules:
  0.0 1338.5 jit_solution(1799674309868129240)
XLA Ops:
  15.1 44.7 %all_to_all.22 = bf16[128,4,1792]{2,0,1:T(8,128)(2,1)S(1)} all-to-all(bf16[128,4,1792]{2,0,1:T(8,128)(2,1)S(1)} %copy.14), channel_id=1, replica_groups=mesh['colony'=8,'fsdp'=4] {'fsdp'}, dimensions={1} | all-to-all | bytes 3670016 | tf_op jit(solution)/shard_map/all_to_all | solution.py:32
  59.8 6.3 all-gather.2.cloned.1.call-done
  66.1 15.8 %fusion.19 = (bf16[512,1792]{1,0:T(8,128)(2,1)S(1)}, f32[512,1792]{1,0:T(8,128)S(1)}) fusion(bf16[128,4,1792]{2,0,1:T(8,128)(2,1)S(1)} %all_to_all.22, bf16[512,4096]{1,0:T(8,128)(2,1)} %all-gather.2.cloned.1.call-done, bf16[4096,1792]{1,0:T(8,128)(2,1)} %param.9), kind=kOutput, calls=%fused_computation.31 | convolution fusion | flops 7522615296 | bytes 26214400 | tf_op jit(solution)/shard_map/dot_general | solution.py:11
  81.9 12.9 fusion.17
  94.9 11.1 fusion.13
  105.9 11.3 fusion.14
  117.3 20.6 %maximum_bitcast_fusion = bf16[1,2,4096,1792]{3,2,1,0:T(8,128)(2,1)} fusion(bf16[1,4096,1792]{2,1,0:T(8,128)(2,1)} %fusion.14, bf16[1,4096,1792]{2,1,0:T(8,128)(2,1)} %fusion.13), kind=kLoop, calls=%fused_computation.18 | loop fusion | flops 14680064 | bytes 58720256 | tf_op jit(solution)/shard_map/broadcast_in_dim | solution.py:36
  137.9 53.1 %copy.15 = bf16[1,2,4096,1792]{3,1,0,2:T(2,128)(2,1)} copy(bf16[1,2,4096,1792]{3,2,1,0:T(8,128)(2,1)} %maximum_bitcast_fusion) | data formatting | bytes 58720256 | tf_op jit(solution)/shard_map/broadcast_in_dim | solution.py:36
  191.0 6.9 all-to-all-start.1
  198.1 633.0 %all-to-all-done.1 = bf16[1,2,4096,1792]{3,1,0,2:T(2,128)(2,1)} async-done(((bf16[1,2,4096,1792]{3,1,0,2:T(2,128)(2,1)}), bf16[1,2,4096,1792]{3,1,0,2:T(2,128)(2,1)}, u32[]{:S(2)}, u32[]{:S(2)}) %all-to-all-start.1) | async-done | bytes 29360160 | tf_op jit(solution)/shard_map/all_to_all | solution.py:37
  831.1 60.1 %fusion.6 = f32[2,512,1792]{2,0,1:T(2,128)S(1)} fusion(bf16[1,2,8,512,1792]{4,1,3,2,0:T(2,128)(2,1)} %bitcast.11, f32[8]{0:T(128)S(1)} %get-tuple-element.4), kind=kLoop, calls=%fused_computation.11 | loop fusion | flops 42205184 | bytes 36700192 | tf_op jit(solution)/shard_map/reduce_sum | solution.py:44
  891.2 57.7 %fusion.12 = f32[8]{0:T(128)S(1)} fusion(bf16[1,2,8,512,1792]{4,1,3,2,0:T(2,128)(2,1)} %bitcast.11, f32[8]{0:T(128)S(1)} %get-tuple-element.5, f32[2,512,1792]{2,0,1:T(2,128)S(1)} %fusion.6), kind=kLoop, calls=%fused_computation.17 | loop fusion | flops 73400312 | bytes 36700224 | tf_op jit(solution)/shard_map/reduce_sum | solution.py:49
  948.9 5.7 psum.42
  954.6 19.6 %psum.43 = f32[8]{0:T(128)S(1)} all-reduce(f32[8]{0:T(128)S(1)} %psum.42), channel_id=1, replica_groups=mesh['colony'=8,'fsdp'=4] {'colony'}, use_global_device_ids=true, to_apply=%region_5.6 | all-reduce | flops 8 | bytes 64 | tf_op jit(solution)/shard_map/psum | solution.py:50
  975.6 60.1 %fusion.7 = f32[2,512,1792]{2,0,1:T(2,128)S(1)} fusion(bf16[1,2,8,512,1792]{4,1,3,2,0:T(2,128)(2,1)} %bitcast.11, f32[8]{0:T(128)S(1)} %multiply_divide_fusion.2), kind=kLoop, calls=%fused_computation.12 | loop fusion | flops 42205184 | bytes 36700192 | tf_op jit(solution)/shard_map/reduce_sum | solution.py:44
  1035.7 57.7 %fusion.11 = f32[8]{0:T(128)S(1)} fusion(bf16[1,2,8,512,1792]{4,1,3,2,0:T(2,128)(2,1)} %bitcast.11, f32[8]{0:T(128)S(1)} %get-tuple-element.5, f32[2,512,1792]{2,0,1:T(2,128)S(1)} %fusion.7), kind=kLoop, calls=%fused_computation.16 | loop fusion | flops 73400312 | bytes 36700224 | tf_op jit(solution)/shard_map/reduce_sum | solution.py:49
  1093.4 5.6 psum.44
  1099.0 17.4 %psum.45 = f32[8]{0:T(128)S(1)} all-reduce(f32[8]{0:T(128)S(1)} %psum.44), channel_id=1, replica_groups=mesh['colony'=8,'fsdp'=4] {'colony'}, use_global_device_ids=true, to_apply=%region_10.11 | all-reduce | flops 8 | bytes 64 | tf_op jit(solution)/shard_map/psum | solution.py:50
  1117.6 60.1 %fusion.8 = f32[2,512,1792]{2,0,1:T(2,128)S(1)} fusion(bf16[1,2,8,512,1792]{4,1,3,2,0:T(2,128)(2,1)} %bitcast.11, f32[8]{0:T(128)S(1)} %multiply_divide_fusion.1), kind=kLoop, calls=%fused_computation.13 | loop fusion | flops 42205184 | bytes 36700192 | tf_op jit(solution)/shard_map/reduce_sum | solution.py:44
  1177.7 57.7 %fusion.10 = f32[8]{0:T(128)S(1)} fusion(bf16[1,2,8,512,1792]{4,1,3,2,0:T(2,128)(2,1)} %bitcast.11, f32[8]{0:T(128)S(1)} %get-tuple-element.5, f32[2,512,1792]{2,0,1:T(2,128)S(1)} %fusion.8), kind=kLoop, calls=%fused_computation.15 | loop fusion | flops 73400312 | bytes 36700224 | tf_op jit(solution)/shard_map/reduce_sum | solution.py:49
  1235.4 5.6 psum.46
  1241.1 19.4 %psum.47 = f32[8]{0:T(128)S(1)} all-reduce(f32[8]{0:T(128)S(1)} %psum.46), channel_id=1, replica_groups=mesh['colony'=8,'fsdp'=4] {'colony'}, use_global_device_ids=true, to_apply=%region_15.16 | all-reduce | flops 8 | bytes 64 | tf_op jit(solution)/shard_map/psum | solution.py:50
  1261.7 60.1 %fusion.9 = f32[2,512,1792]{2,0,1:T(2,128)S(1)} fusion(bf16[1,2,8,512,1792]{4,1,3,2,0:T(2,128)(2,1)} %bitcast.11, f32[8]{0:T(128)S(1)} %multiply_divide_fusion), kind=kLoop, calls=%fused_computation.14 | loop fusion | flops 42205184 | bytes 36700192 | tf_op jit(solution)/shard_map/reduce_sum | solution.py:44
  1321.8 5.8 fusion.26
  (23 shorter events, 15.3 us)
Async XLA Ops:
  7.2 58.9 %all-gather.2.cloned.1.call-start = ((), (), s32[]{:S(2)}) async-start(), calls=%async_computation.2 | async-start | bytes 5242880 | tf_op jit(solution)/shard_map/all_gather | solution.py:31
  66.1 15.8 %copy-start = (bf16[512,4096]{1,0:T(8,128)(2,1)S(1)}, bf16[512,4096]{1,0:T(8,128)(2,1)}, u32[]{:S(2)}) copy-start(bf16[512,4096]{1,0:T(8,128)(2,1)} %all-gather.2.cloned.1.call-done) | copy-start | bytes 12582916
  191.0 6.9 copy-start.1
  191.0 6.9 copy-start.2
  191.0 640.1 %all-to-all-start.1 = ((bf16[1,2,4096,1792]{3,1,0,2:T(2,128)(2,1)}), bf16[1,2,4096,1792]{3,1,0,2:T(2,128)(2,1)}, u32[]{:S(2)}, u32[]{:S(2)}) async-start(bf16[1,2,4096,1792]{3,1,0,2:T(2,128)(2,1)} %copy.15), calls=%async_computation.1 | async-start | bytes 58720256 | tf_op jit(solution)/shard_map/all_to_all | solution.py:37
Sparse Core Ops, SparseCore 0:
  11.4 54.6 all-gather.1
